TPU v7x, 256 devices: a whole 4x4x8 slice. The times are simulated.
256 devices in a mesh: ex: 32 (over x_hi, z, core), layer: 8 (over x_lo, y).
Axes of the slice: x: 4 (x_hi: 2, x_lo: 2; x = x_hi * 2 + x_lo), y: 4, z: 8, core: 2. Of those that a mesh axis runs over, the one named last changes fastest.
Arguments:
- train_grads: bfloat16 [16384, 8, 8192], P('ex', 'layer'), may hold values from -6 to 6
- query_grads: bfloat16 [1024, 8, 8192], P('ex', 'layer'), may hold values from -6 to 6
- left_factor: float32 [8, 64, 64], P('layer'), may hold values from -0.4 to 0.4
- right_factor: float32 [8, 128, 128], P('layer'), may hold values from -0.3 to 0.3
- query_order: int32 [1024], replicated, may hold values from 0 to 1023, each once
Outputs:
- scores: float32 [16384, 1024], P('ex', 'layer')
Inputs may be any that keep to these rules, and one draw needn't show every extreme that they name: `query_order`: each query index appears exactly once.
All inputs are finite; a program needn't handle non-finite values.
Results may differ from a plain program's by a relative error of at most 0.0059.
Values may be sent and summed in bfloat16 or wider, within the bound.
A program may use at most 128 MiB of HBM per device.

v0:
```python
import jax
import jax.numpy as jnp
from jax import lax
from jax.sharding import PartitionSpec as P

FA = 64
FB = 128


def condition(block, left, right):
    count = block.shape[0]
    left_mat = (jnp.eye(FA, dtype=jnp.float32) + left).astype(jnp.bfloat16)
    right_mat = (jnp.eye(FB, dtype=jnp.float32) + right).astype(jnp.bfloat16)
    flat = block.reshape(count * FA, FB)
    mid = jnp.dot(flat, right_mat, preferred_element_type=jnp.float32).astype(jnp.bfloat16)
    mid = mid.reshape(count, FA, FB)
    out = jnp.einsum("ab,qbc->qac", left_mat, mid, preferred_element_type=jnp.float32)
    return out.reshape(count, FA * FB).astype(jnp.bfloat16)


def local(train_grads, query_grads, left_factor, right_factor, query_order):
    grads = train_grads[:, 0, :]
    raw = query_grads[:, 0, :]
    left = left_factor[0]
    right = right_factor[0]
    layer_count = left_factor.shape[0] * lax.axis_size("layer")
    factor = jnp.sqrt(jnp.float32(grads.shape[1] * layer_count))
    outgoing = condition(raw, left, right)
    tile = lax.dot_general(
        grads,
        lax.all_gather(outgoing, "ex", axis=0, tiled=True),
        (((1,), (1,)), ((), ())),
        preferred_element_type=jnp.float32,
    )
    picked = jnp.take(tile, query_order, axis=1)
    summed = lax.psum_scatter(picked, "layer", scatter_dimension=1, tiled=True)
    return summed / factor


def solution(mesh):
    return jax.shard_map(
        local,
        mesh=mesh,
        in_specs=(
            P("ex", "layer", None),
            P("ex", "layer", None),
            P("layer", None, None),
            P("layer", None, None),
            P(),
        ),
        out_specs=P("ex", "layer"),
        check_vma=False,
    )
```

profile of v0, /device:TPU:4, one launch (start us, length us, event | category | flops | bytes accessed | tf_op | source)
XLA Modules:
  0.0 224.5 jit_solution(13229453137052629978)
XLA Ops:
  6.5 0.0 copy-start
  6.5 0.0 all-gather.2.cloned.1.call-start
  6.5 1.3 reshape_squeeze.3
  7.8 1.2 fusion.2
  9.0 0.0 copy-start.1
  9.0 0.3 copy.8
  9.3 0.0 copy-done
  9.3 0.3 convolution_convert_fusion.1
  9.6 1.1 copy.12
  10.7 0.0 all-gather.2.cloned.1.call-update
  10.8 0.0 reduce-scatter.2.cloned.1.call-start
  10.8 0.0 copy-done.1
  10.9 138.3 %all-gather.2.cloned.1.call-done = bf16[1024,8192]{1,0:T(8,128)(2,1)} async-done(((bf16[32,8192]{1,0:T(8,128)(2,1)}), bf16[1024,8192]{1,0:T(8,128)(2,1)}) %all-gather.2.cloned.1.call-update) | async-done | bytes 16777232 | tf_op jit(solution)/shard_map/all_gather | solution.py:31
  149.2 14.4 %fusion.3 = f32[512,1024]{0,1:T(8,128)S(1)} fusion(bf16[1024,8192]{1,0:T(8,128)(2,1)} %all-gather.2.cloned.1.call-done, bf16[512,1,8192]{2,0,1:T(8,128)(2,1)} %param.5), kind=kOutput, calls=%fused_computation.6 | convolution fusion | flops 8589934592 | bytes 27262976 | tf_op jit(solution)/shard_map/dot_general | solution.py:29
  163.6 4.9 %gather_fusion = f32[1024,512]{1,0:T(8,128)} fusion(f32[512,1024]{0,1:T(8,128)S(1)} %fusion.3, s32[1024]{0:T(1024)S(1)} %fusion.10), kind=kCustom, calls=%fused_computation | custom fusion | bytes 4198400 | tf_op jit(solution)/shard_map/jit(_take)/gather | solution.py:35
  168.5 3.2 %select_bitcast_fusion = f32[512,1024]{0,1:T(8,128)} fusion(f32[1024,512]{1,0:T(8,128)} %gather_fusion, pred[1024]{0:T(1024)(128)(4,1)S(1)} %compare_and_fusion), kind=kLoop, calls=%fused_computation.5 | loop fusion | flops 524288 | bytes 4195328 | tf_op jit(solution)/shard_map/jit(_take)/select_n | solution.py:35
  171.6 0.0 reduce-scatter.2.cloned.1.call-update
  171.7 44.2 %reduce-scatter.2.cloned.1.call-done = f32[512,128]{0,1:T(8,128)} async-done(((f32[512,1024]{0,1:T(8,128)}), f32[512,128]{0,1:T(8,128)}) %reduce-scatter.2.cloned.1.call-update) | async-done | bytes 262160 | tf_op jit(solution)/shard_map/reduce_scatter | solution.py:36
  215.8 1.0 broadcast_multiply_fusion
  216.8 0.8 copy.9
  (2 shorter events, 0.0 us)
Async XLA Ops:
  6.5 2.8 %copy-start = (f32[1,64,64]{2,1,0:T(8,128)S(1)}, f32[1,64,64]{2,1,0:T(8,128)}, u32[]{:S(2)}) copy-start(f32[1,64,64]{2,1,0:T(8,128)} %param.7) | copy-start | bytes 49156
  6.5 142.7 %all-gather.2.cloned.1.call-start = ((), (), s32[]{:S(2)}) async-start(), calls=%async_computation.1 | async-start | bytes 17301504 | tf_op jit(solution)/shard_map/all_gather | solution.py:31
  9.0 1.8 copy-start.1
  10.8 205.1 %reduce-scatter.2.cloned.1.call-start = ((), (), s32[]{:S(2)}) async-start(), calls=%async_computation.2 | async-start | bytes 2359296 | tf_op jit(solution)/shard_map/reduce_scatter | solution.py:36
Sparse Core Ops, SparseCore 0:
  10.9 138.2 all-gather.1
  171.8 43.9 reduce-scatter.1
where the time goes:
time: 225 us; the launch traced here: 224 us
  waiting for transfers between devices  183 us (81%)
  matrix products  15.9 us (7%)
  between operations  13.5 us (6%)
  local copies, waits for them, and re-layouts  8.43 us (4%)
  other arithmetic  4.13 us (2%)
    all_gather x1, waiting for transfers between devices, local(): lax.all_gather(outgoing, 'ex', axis=0, tiled=True)  138 us
    reduce_scatter x1, waiting for transfers between devices, local(): summed = lax.psum_scatter(picked, 'layer', scatter_dimension=1, tiled=True)  44.2 us
    dot_general x1, matrix products, local(): lax.dot_general(grads, lax.all_gather(outgoing, 'ex', axis=0, tiled=True)...  14.4 us
    gather x1, local copies, waits for them, and re-layouts, local(): picked = jnp.take(tile, query_order, axis=1)  4.85 us
  transfers between devices with their start and end apart: 2, of which 2 were waited for; matrix products, arithmetic and copies ran while one was open for 0% of the time, Pallas kernels for 0%

commit v1 on v0

v1 whole, which is shorter than its diff:
```python
import functools

import jax
import jax.numpy as jnp
from jax import lax
from jax.experimental import pallas as pl
from jax.experimental.pallas import tpu as pltpu
from jax.sharding import PartitionSpec as P

FA = 64
FB = 128
MESH = pl.DeviceIdType.MESH

Z = 8
GROUP = 8
SLOTS = 16
PART = 4
Q_PARTS = (0, 1)
P_PARTS = (2, 3)
FWD, BWD = 0, 1
LAST = 4
REACH = {0: (4, 3), 1: (3, 4), 2: (4, 3), 3: (3, 4)}


def slot_of(step, way, other):
    if step == 0:
        return other
    if step == LAST:
        return 14 + other
    return 2 + 4 * (step - 1) + 2 * other + way


BATCHES = ((0, 2), (2, 4), (6, 4), (10, 4), (14, 2))


def kernel(cond_ref, grads_ref, order_ref, out_ref, grads, block, acc, tile, pick, inbox, outbox, final,
           load_sem, main_recv, z_send, zb_send, x_send, sib_send, sib_recv, red_send, red_recv, fin_send, fin_recv):
    ex, me = lax.axis_index("ex"), lax.axis_index("layer")
    core = lax.rem(ex, 2)
    z = lax.rem(ex // 2, Z)
    hi = ex // (2 * Z)
    wide = block.shape[3] // PART

    def at(h, zz, c):
        return h * (2 * Z) + zz * 2 + c

    z_next = (at(hi, lax.rem(z + 1, Z), core), me)
    z_prev = (at(hi, lax.rem(z + Z - 1, Z), core), me)
    across = (at(1 - hi, z, core), me)
    sibling = (at(hi, z, 1 - core), me)
    peers = [(ex, lax.rem(me + j, GROUP)) for j in range(1, GROUP)]

    load = pltpu.make_async_copy(grads_ref, grads, load_sem)
    load.start()

    barrier = pltpu.get_barrier_semaphore()
    partners = [z_next, z_prev, across, sibling] + peers
    for d in partners:
        pl.semaphore_signal(barrier, inc=1, device_id=d, device_id_type=MESH)

    block[0, core] = cond_ref[...]
    for s in range(SLOTS):
        step = 0 if s < 2 else LAST if s >= 14 else 1 + (s - 2) // 4
        other = s % 2 if s < 2 or s >= 14 else ((s - 2) // 2) % 2
        way = 0 if s < 2 or s >= 14 else (s - 2) % 2
        zz = lax.rem(z + (Z - step if way == FWD else step), Z)
        hh = 1 - hi if other else hi
        first = (hh * Z + zz) * 64
        ids = first + lax.broadcasted_iota(jnp.int32, (64, pick.shape[1]), 0)
        pick[s * 64:(s + 1) * 64, :] = jnp.where(ids == order_ref[...], 1.0, 0.0).astype(jnp.bfloat16)

    pl.semaphore_wait(barrier, len(partners))

    def chunk(s, c, k):
        return block.at[s, c, :, pl.ds(k * wide, wide)]

    sent = []

    def send(s, to, k, device, send_sem, recv_sem):
        copy = pltpu.make_async_remote_copy(
            src_ref=chunk(s, core, k), dst_ref=chunk(to, core, k), send_sem=send_sem, recv_sem=recv_sem,
            device_id=device, device_id_type=MESH)
        copy.start()
        sent.append(copy)

    def send_z(step, way, other, k):
        s, to = slot_of(step, way, other), slot_of(step + 1, way, other)
        if way == FWD:
            send(s, to, k, z_next, z_send.at[s, k], main_recv.at[to, k])
        else:
            send(s, to, k, z_prev, zb_send.at[s, k] if step == 0 else z_send.at[s, k], main_recv.at[to, k])

    def send_x(step, way, k):
        s, to = slot_of(step, way, 0), slot_of(step, way, 1)
        send(s, to, k, across, x_send.at[s, k], main_recv.at[to, k])

    def send_sib(s, k):
        send(s, s, k, sibling, sib_send.at[s, k], sib_recv.at[s, k])

    def wait_main(s, k):
        pltpu.make_async_remote_copy(
            src_ref=chunk(s, core, k), dst_ref=chunk(s, core, k), send_sem=z_send.at[s, k],
            recv_sem=main_recv.at[s, k], device_id=sibling, device_id_type=MESH).wait_recv()

    def wait_sib(s, k):
        pltpu.make_async_remote_copy(
            src_ref=chunk(s, 1 - core, k), dst_ref=chunk(s, 1 - core, k), send_sem=sib_send.at[s, k],
            recv_sem=sib_recv.at[s, k], device_id=sibling, device_id_type=MESH).wait_recv()

    def compute(b):
        first, count = BATCHES[b]
        for s in range(first, first + count):
            for k in range(PART):
                wait_sib(s, k)
        if b == 0:
            load.wait()
        w = count * 64
        acc[:, :w] = jnp.zeros((acc.shape[0], w), jnp.float32)

        @pl.loop(0, PART)
        def _(i):
            cols = pl.ds(pl.multiple_of(i * wide, wide), wide)
            rhs = block[first:first + count, :, :, cols].reshape(w, wide)
            acc[:, :w] += lax.dot_general(grads[:, cols], rhs, (((1,), (1,)), ((), ())),
                                          preferred_element_type=jnp.float32)

        at_cols = slice(first * 64, first * 64 + w)
        tile[:, at_cols] = acc[:, :w].astype(jnp.bfloat16)
        for j, peer in enumerate(peers):
            rows = pl.ds(pl.multiple_of(peer[1] * 64, 64), 64)
            copy = pltpu.make_async_remote_copy(
                src_ref=tile.at[rows, at_cols], dst_ref=inbox.at[j, :, at_cols],
                send_sem=red_send.at[b, j], recv_sem=red_recv.at[b, j], device_id=peer, device_id_type=MESH)
            copy.start()
            reduces.append(copy)

    reduces = []

    for k in P_PARTS:
        send_x(0, 0, k)
    for k in range(PART):
        send_z(0, FWD, 0, k)
        send_z(0, BWD, 0, k)
    for k in range(PART):
        send_sib(0, k)
    for k in P_PARTS:
        wait_main(1, k)
        send_z(0, FWD, 1, k)
        send_z(0, BWD, 1, k)
        send_sib(1, k)
    for k in Q_PARTS:
        send_x(0, 0, k)

    for step in range(1, LAST + 1):
        for k, other in ((0, 0), (1, 0), (2, 0), (3, 0), (2, 1), (3, 1)):
            for way in (FWD, BWD):
                if REACH[k][way] < step:
                    continue
                s = slot_of(step, way, other)
                wait_main(s, k)
                if REACH[k][way] > step:
                    send_z(step, way, other, k)
                if k in Q_PARTS:
                    send_x(step, way, k)
                send_sib(s, k)
            if k == 1:
                for w in (FWD, BWD) if step > 1 else (FWD,):
                    for q in Q_PARTS:
                        s = slot_of(step - 1, w, 1)
                        wait_main(s, q)
                        send_sib(s, q)
                compute(step - 1)
    for q in Q_PARTS:
        s = slot_of(LAST, 0, 1)
        wait_main(s, q)
        send_sib(s, q)
    compute(LAST)

    for copy in reduces:
        copy.wait_recv()
    total = tile[pl.ds(pl.multiple_of(me * 64, 64), 64), :].astype(jnp.float32)
    for j in range(GROUP - 1):
        total += inbox[j].astype(jnp.float32)
    total = total * (1.0 / 256.0)
    high = total.astype(jnp.bfloat16)
    low = (total - high.astype(jnp.float32)).astype(jnp.bfloat16)
    scores = jnp.dot(high, pick[...], preferred_element_type=jnp.float32)
    scores += jnp.dot(low, pick[...], preferred_element_type=jnp.float32)
    for m in range(GROUP):
        outbox[m] = scores[:, m * 128:(m + 1) * 128]
    finals = []
    for j, peer in enumerate(peers):
        copy = pltpu.make_async_remote_copy(
            src_ref=outbox.at[peer[1]], dst_ref=final.at[me], send_sem=fin_send.at[j], recv_sem=fin_recv.at[j],
            device_id=peer, device_id_type=MESH)
        copy.start()
        finals.append(copy)
    final[me] = outbox[me]
    for copy in sent:
        copy.wait_send()
    for copy in reduces:
        copy.wait_send()
    for copy in finals:
        copy.wait()
    out_ref[...] = final[...].reshape(out_ref.shape)


def condition(block, left, right):
    count = block.shape[0]
    left_mat = (jnp.eye(FA, dtype=jnp.float32) + left).astype(jnp.bfloat16)
    right_mat = (jnp.eye(FB, dtype=jnp.float32) + right).astype(jnp.bfloat16)
    flat = block.reshape(count * FA, FB)
    mid = jnp.dot(flat, right_mat, preferred_element_type=jnp.float32).astype(jnp.bfloat16)
    mid = mid.reshape(count, FA, FB)
    out = jnp.einsum("ab,qbc->qac", left_mat, mid, preferred_element_type=jnp.float32)
    return out.reshape(count, FA * FB).astype(jnp.bfloat16)


def local(train_grads, query_grads, left_factor, right_factor, query_order):
    grads = train_grads[:, 0, :]
    outgoing = condition(query_grads[:, 0, :], left_factor[0], right_factor[0])
    rows, depth = grads.shape
    own = outgoing.shape[0]
    queries = query_order.shape[0]
    dma = pltpu.SemaphoreType.DMA
    return pl.pallas_call(
        kernel,
        name="scores",
        out_shape=jax.ShapeDtypeStruct((rows, queries // GROUP), jnp.float32),
        in_specs=[
            pl.BlockSpec(memory_space=pltpu.VMEM),
            pl.BlockSpec(memory_space=pl.ANY),
            pl.BlockSpec(memory_space=pltpu.VMEM),
        ],
        out_specs=pl.BlockSpec(memory_space=pltpu.VMEM),
        scratch_shapes=[
            pltpu.VMEM((rows, depth), jnp.bfloat16),
            pltpu.VMEM((SLOTS, 2, own, depth), jnp.bfloat16),
            pltpu.VMEM((rows, 256), jnp.float32),
            pltpu.VMEM((rows, queries), jnp.bfloat16),
            pltpu.VMEM((queries, queries), jnp.bfloat16),
            pltpu.VMEM((GROUP - 1, rows // GROUP, queries), jnp.bfloat16),
            pltpu.VMEM((GROUP, rows // GROUP, queries // GROUP), jnp.float32),
            pltpu.VMEM((GROUP, rows // GROUP, queries // GROUP), jnp.float32),
            dma,
            dma((SLOTS, PART)),
            dma((SLOTS, PART)),
            dma((2, PART)),
            dma((SLOTS, PART)),
            dma((SLOTS, PART)),
            dma((SLOTS, PART)),
            dma((len(BATCHES), GROUP - 1)),
            dma((len(BATCHES), GROUP - 1)),
            dma((GROUP - 1,)),
            dma((GROUP - 1,)),
        ],
        compiler_params=pltpu.CompilerParams(
            collective_id=0, has_side_effects=True, vmem_limit_bytes=48 * 2**20
        ),
        cost_estimate=pl.CostEstimate(
            flops=2 * rows * depth * queries, bytes_accessed=rows * depth * 2, transcendentals=0
        ),
    )(outgoing, grads, query_order.reshape(1, queries))


def solution(mesh):
    return jax.shard_map(
        local,
        mesh=mesh,
        in_specs=(
            P("ex", "layer", None),
            P("ex", "layer", None),
            P("layer", None, None),
            P("layer", None, None),
            P(),
        ),
        out_specs=P("ex", "layer"),
        check_vma=False,
    )
```

time: 225 us -> 95.5 us (0.42)
  waiting for transfers between devices: 183 us -> 0 us
  Pallas kernels: 0 us -> 88.2 us
  matrix products: 15.9 us -> 2.2 us
  between operations: 13.5 us -> 0.05 us
  local copies, waits for them, and re-layouts: 8.43 us -> 3.28 us
  other arithmetic: 4.13 us -> 0 us
    all_gather x1 -> x0, waiting for transfers between devices: 138 us -> none  [local(): lax.all_gather(outgoing, 'ex', axis=0, tiled=True)]
    pallas_call x0 -> x1, Pallas kernels: none -> 88.2 us  [local(): pl.pallas_call(kernel, name='scores', out_shape=jax.ShapeDtypeStruct((row...]
    reduce_scatter x1 -> x0, waiting for transfers between devices: 44.2 us -> none  [local(): summed = lax.psum_scatter(picked, 'layer', scatter_dimension=1, tiled=True)]
    dot_general x1 -> x0, matrix products: 14.4 us -> none  [local(): lax.dot_general(grads, lax.all_gather(outgoing, 'ex', axis=0, tiled=True)...]
    gather x1 -> x0, local copies, waits for them, and re-layouts: 4.85 us -> none  [local(): picked = jnp.take(tile, query_order, axis=1)]
    select_n x1 -> x0, other arithmetic: 3.15 us -> none  [local(): picked = jnp.take(tile, query_order, axis=1)]
  transfers between devices with their start and end apart: 2 -> 0, of which waited for: 2 -> 0; matrix products, arithmetic and copies ran while one was open for 0% -> 0% of each run, Pallas kernels for 0% -> 0%
where the time goes in v1:
time: 95.5 us; the launch traced here: 93.7 us
  Pallas kernels  88.2 us (92%)
  local copies, waits for them, and re-layouts  3.28 us (3%)
  matrix products  2.2 us (2%)
    pallas_call x1, Pallas kernels, local(): pl.pallas_call(kernel, name='scores', out_shape=jax.ShapeDtypeStruct((row...  88.2 us

profile of v1, /device:TPU:4, one launch (start us, length us, event | category | flops | bytes accessed | tf_op | source)
XLA Modules:
  0.0 93.7 jit_solution(5037243937392529783)
XLA Ops:
  0.0 1.3 %reshape_squeeze.3 = bf16[2048,128]{1,0:T(8,128)(2,1)S(1)} reshape(bf16[32,1,8192]{2,0,1:T(8,128)(2,1)} %param.6) | data formatting | bytes 1048576 | tf_op jit(solution)/shard_map/reshape;squeeze | solution.py:212
  1.3 1.2 %fusion = bf16[2048,128]{0,1:T(8,128)(2,1)S(1)} fusion(bf16[2048,128]{1,0:T(8,128)(2,1)S(1)} %reshape_squeeze.3, f32[1,128,128]{2,1,0:T(8,128)} %param.8), kind=kOutput, calls=%fused_computation.1 | convolution fusion | flops 67436544 | bytes 1114112 | tf_op jit(solution)/shard_map/dot_general | solution.py:213
  2.5 0.3 copy.7
  2.7 1.0 %convolution_convert_fusion.1 = bf16[32,128,64]{1,2,0:T(8,128)(2,1)S(1)} fusion(bf16[32,64,128]{2,1,0:T(8,128)(2,1)S(1)} %bitcast.23, f32[1,64,64]{2,1,0:T(8,128)} %param.7), kind=kOutput, calls=%fused_computation.2 | convolution fusion | flops 33832960 | bytes 1064960 | tf_op jit(solution)/shard_map/ab,qbc->qac/dot_general | solution.py:215
  3.8 0.3 copy.10
  4.1 0.0 copy-start
  4.1 0.7 copy-done
  4.8 88.2 %scores.1 = f32[512,128]{1,0:T(8,128)S(1)} custom-call(bf16[32,8192]{1,0:T(8,128)(2,1)S(1)} %bitcast.21, bf16[512,8192]{1,0:T(8,128)(2,1)} %bitcast.25, s32[1,1024]{1,0:T(1,128)S(1)} %bitcast.22), custom_call_target="tpu_custom_call" | custom-call | flops 8589934592 | bytes 8388608 | tf_op jit(solution)/shard_map/scores/pallas_call | solution.py:226
  93.0 0.7 copy.12
Async XLA Ops:
  4.1 0.7 copy-start

commit v2 on v0

v2 whole, which is shorter than its diff:
```python
import functools

import jax
import jax.numpy as jnp
from jax import lax
from jax.experimental import pallas as pl
from jax.experimental.pallas import tpu as pltpu
from jax.sharding import PartitionSpec as P

FA = 64
FB = 128
MESH = pl.DeviceIdType.MESH

Z = 8
GROUP = 8
FWD, BWD = 0, 1
LAST = 4

NEAR, WIDE = 0, 1
QUARTERS = 4

SLOTS = 16
FIRST = 14

ARRIVALS = 34
OWN_NEAR, OWN_WIDE, THEIR_WIDE, THEIR_NEAR = range(4)


def slot_of(step, way, other):
    return 2 + 4 * (step - 1) + 2 * other + way


def arrival(step, way, what):
    return 2 + 8 * (step - 1) + 4 * way + what


def eye_plus(mat):
    n = mat.shape[0]
    rows = lax.broadcasted_iota(jnp.int32, (n, n), 0)
    cols = lax.broadcasted_iota(jnp.int32, (n, n), 1)
    return (jnp.where(rows == cols, 1.0, 0.0) + mat).astype(jnp.bfloat16)


def condition(raw, left, right, by_row, by_query, out):
    count = raw.shape[0]
    left_mat, right_mat = eye_plus(left[...]), eye_plus(right[...])
    group = 16
    for a in range(0, FA, group):
        rows = jnp.concatenate([raw[:, i * FB:(i + 1) * FB] for i in range(a, a + group)], axis=0)
        mid = jnp.dot(rows, right_mat, preferred_element_type=jnp.float32).astype(jnp.bfloat16).astype(jnp.float32)
        for i in range(group):
            by_query[pl.ds(a + i, count, stride=FA), :] = mid[i * count:(i + 1) * count, :]
    group = 8
    for q in range(0, count, group):
        mid = jnp.concatenate([by_query[i * FA:(i + 1) * FA, :] for i in range(q, q + group)], axis=1)
        done = jnp.dot(left_mat, mid.astype(jnp.bfloat16), preferred_element_type=jnp.float32)
        for i in range(group):
            by_row[pl.ds(q + i, FA, stride=count), :] = done[:, i * FB:(i + 1) * FB]
    for a in range(FA):
        out[:, a * FB:(a + 1) * FB] = by_row[a * count:(a + 1) * count, :].astype(jnp.bfloat16)


def kernel(raw_ref, grads_ref, left_ref, right_ref, order_ref, out_ref, raw, left, right, order, by_row, by_query,
           grads, block, acc, tile, pick, scores, inbox, outbox, final,
           load_sem, main_recv, z_send, x_send, sib_send, sib_recv, red_send, red_recv, fin_send, fin_recv):
    ex, me = lax.axis_index("ex"), lax.axis_index("layer")
    core = lax.rem(ex, 2)
    z = lax.rem(ex // 2, Z)
    hi = ex // (2 * Z)
    depth = block.shape[3]
    half, quarter = depth // 2, depth // QUARTERS

    def at(h, zz, c):
        return h * (2 * Z) + zz * 2 + c

    z_next = (at(hi, lax.rem(z + 1, Z), core), me)
    z_prev = (at(hi, lax.rem(z + Z - 1, Z), core), me)
    toward = (z_next, z_prev)
    across = (at(1 - hi, z, core), me)
    sibling = (at(hi, z, 1 - core), me)

    def peer_of(j):
        return ex, lax.rem(me + j + 1, GROUP)

    loads = [pltpu.make_async_copy(src, dst, load_sem.at[i]) for i, (src, dst) in enumerate(
        ((raw_ref, raw), (right_ref, right), (left_ref, left), (order_ref, order), (grads_ref, grads)))]
    for load in loads[:4]:
        load.start()

    barrier = pltpu.get_barrier_semaphore()
    for d in (z_next, z_prev, across, sibling):
        pl.semaphore_signal(barrier, inc=1, device_id=d, device_id_type=MESH)

    @pl.loop(0, GROUP - 1)
    def _(j):
        pl.semaphore_signal(barrier, inc=1, device_id=peer_of(j), device_id_type=MESH)

    for load in loads[:3]:
        load.wait()
    condition(raw, left, right, by_row, by_query, block.at[0, core])
    loads[4].start()
    pl.semaphore_wait(barrier, 4 + GROUP - 1)

    def part(s, c, start, width):
        return block.at[s, c, :, pl.ds(start, width)]

    def remote(src, dst, send_sem, recv_sem, device):
        return pltpu.make_async_remote_copy(src_ref=src, dst_ref=dst, send_sem=send_sem, recv_sem=recv_sem,
                                            device_id=device, device_id_type=MESH)

    def send_z(step, way, s, to, start, width, signal):
        remote(part(s, core, start, width), part(to, core, start, width), z_send.at[step], main_recv.at[signal],
               toward[way]).start()

    def send_x(step, s, to, start, width, signal):
        remote(part(s, core, start, width), part(to, core, start, width), x_send.at[step], main_recv.at[signal],
               across).start()

    def send_sib(batch, s, start, width):
        remote(part(s, core, start, width), part(s, core, start, width), sib_send.at[batch], sib_recv.at[batch],
               sibling).start()

    def arrived(s, start, width, signal):
        here = part(s, core, start, width)
        remote(here, here, z_send.at[0], main_recv.at[signal], sibling).wait_recv()

    def sib_batch(batch, first, count, start, width):
        here = block.at[pl.ds(first, count), 1 - core, :, pl.ds(start, width)]
        return remote(here, here, sib_send.at[batch], sib_recv.at[batch], sibling)

    def multiply(first, count, k):
        w = count * 64
        cols = pl.ds(pl.multiple_of(k * quarter, quarter), quarter)
        rhs = block[pl.ds(first, count), :, :, cols].reshape(w, quarter)
        acc[:, :w] += lax.dot_general(grads[:, cols], rhs, (((1,), (1,)), ((), ())),
                                      preferred_element_type=jnp.float32)

    def clear():
        acc[...] = jnp.zeros_like(acc)

    def pass_on(b, start, width, kind):
        tile[:, pl.ds(start, width)] = acc[:, :width].astype(jnp.bfloat16)

        @pl.loop(0, GROUP - 1)
        def _(j):
            peer = peer_of(j)
            rows, cols = pl.ds(pl.multiple_of(peer[1] * 64, 64), 64), pl.ds(start, width)
            remote(tile.at[rows, cols], inbox.at[j, :, cols], red_send.at[b], red_recv.at[kind], peer).start()

    def reduced(b, kind, start, width):
        here = inbox.at[:, :, pl.ds(start, width)]
        return remote(here, here, red_send.at[b], red_recv.at[kind], sibling)

    def batch(b):
        first = slot_of(b, 0, 0)
        sib_batch(b, first, 4, 0, depth).wait_recv()
        clear()

        @pl.loop(0, QUARTERS)
        def _(k):
            multiply(first, 4, k)
        start = 128 + 256 * (b - 1)
        pass_on(b, start if isinstance(b, int) else pl.multiple_of(start, 128), 256, 0)

    send_x(0, 0, 1, half, half, 0)
    for what, start in ((OWN_NEAR, 0), (OWN_WIDE, half)):
        for way in (FWD, BWD):
            send_z(0, way, 0, slot_of(1, way, 0), start, half, arrival(1, way, what))
    send_sib(0, 0, 0, depth)
    clear()
    loads[3].wait()

    @pl.loop(0, SLOTS)
    def _(i):
        edge = (i < 2) | (i >= FIRST)
        step = (i + 2) // 4
        other = jnp.where(edge, lax.rem(i, 2), lax.rem((i + 2) // 2, 2))
        back = jnp.where(edge, 0, lax.rem(i, 2))
        zz = lax.rem(z + jnp.where(back == 1, step, Z - step), Z)
        hh = jnp.where(other == 1, 1 - hi, hi)
        ids = (hh * Z + zz) * 64 + lax.broadcasted_iota(jnp.int32, (64, pick.shape[1]), 0)
        pick[pl.ds(pl.multiple_of(i * 64, 64), 64), :] = jnp.where(ids == order[...], 1.0, 0.0).astype(jnp.bfloat16)

    arrived(1, half, half, 0)
    for way in (FWD, BWD):
        send_z(0, way, 1, slot_of(1, way, 1), half, half, arrival(1, way, THEIR_WIDE))
    send_sib(0, 1, half, half)
    send_x(0, 0, 1, 0, half, 1)
    loads[4].wait()

    @pl.loop(1, LAST)
    def _(step):
        def arrive(what, other, start):
            for way in (FWD, BWD):
                s = slot_of(step, way, other)
                arrived(s, start, half, arrival(step, way, what))

                @pl.when(step < LAST - 1)
                def _():
                    send_z(step, way, s, slot_of(step + 1, way, other), start, half, arrival(step + 1, way, what))

                @pl.when(step == LAST - 1)
                def _():
                    k = start // quarter + way
                    send_z(step, way, s, FIRST + other, k * quarter, quarter, 26 + 4 * other + k)

                if what == OWN_NEAR:
                    send_x(step, s, slot_of(step, way, 1), start, half, arrival(step, way, THEIR_NEAR))
                send_sib(step, s, start, half)

        arrive(OWN_NEAR, 0, 0)

        @pl.when(step == 1)
        def _():
            arrived(1, 0, half, 1)
            send_sib(0, 1, 0, half)
            sib_batch(0, 0, 2, 0, depth).wait_recv()

            @pl.loop(0, QUARTERS)
            def _(k):
                multiply(0, 2, k)
            pass_on(0, 0, 128, 0)

        @pl.when(step > 1)
        def _():
            for way in (FWD, BWD):
                s = slot_of(step - 1, way, 1)
                arrived(s, 0, half, arrival(step - 1, way, THEIR_NEAR))
                send_sib(step - 1, s, 0, half)
            batch(step - 1)

        arrive(OWN_WIDE, 0, half)
        arrive(THEIR_WIDE, 1, half)

    for k in (0, 1):
        arrived(FIRST, k * quarter, quarter, 26 + k)
        send_x(LAST, FIRST, FIRST + 1, k * quarter, quarter, 30 + k)
        send_sib(LAST + k, FIRST, k * quarter, quarter)
    for way in (FWD, BWD):
        s = slot_of(LAST - 1, way, 1)
        arrived(s, 0, half, arrival(LAST - 1, way, THEIR_NEAR))
        send_sib(LAST - 1, s, 0, half)
    batch(LAST - 1)
    clear()
    for k in (2, 3):
        arrived(FIRST, k * quarter, quarter, 26 + k)
        send_sib(LAST + k, FIRST, k * quarter, quarter)
    for k in (0, 1):
        arrived(FIRST + 1, k * quarter, quarter, 30 + k)
        send_sib(LAST + k, FIRST + 1, k * quarter, quarter)

    @pl.loop(0, 2)
    def _(k):
        sib_batch(LAST + k, FIRST, 2, pl.multiple_of(k * quarter, quarter), quarter).wait_recv()
        multiply(FIRST, 2, k)
    for k in (2, 3):
        arrived(FIRST + 1, k * quarter, quarter, 30 + k)
        send_sib(LAST + k, FIRST + 1, k * quarter, quarter)

    mine = pl.ds(pl.multiple_of(me * 64, 64), 64)

    def ordered(start, width):
        total = tile[mine, start:start + width].astype(jnp.float32)
        for j in range(GROUP - 1):
            total += inbox[j, :, start:start + width].astype(jnp.float32)
        total = total * (1.0 / 256.0)
        high = total.astype(jnp.bfloat16)
        low = (total - high.astype(jnp.float32)).astype(jnp.bfloat16)
        both = jnp.dot(jnp.concatenate([high, low], axis=0), pick[start:start + width, :],
                       preferred_element_type=jnp.float32)
        return both[:64] + both[64:]

    early = FIRST * 64
    reduced(0, 0, 0, early).wait_recv()
    scores[...] = ordered(0, early)

    @pl.loop(2, QUARTERS)
    def _(k):
        sib_batch(LAST + k, FIRST, 2, pl.multiple_of(k * quarter, quarter), quarter).wait_recv()
        multiply(FIRST, 2, k)
    pass_on(LAST, early, 128, 1)
    reduced(LAST, 1, early, 128).wait_recv()
    done = (scores[...] + ordered(early, 128)).astype(jnp.bfloat16)
    for m in range(GROUP):
        outbox[m] = done[:, m * 128:(m + 1) * 128]

    @pl.loop(0, GROUP - 1)
    def _(j):
        peer = peer_of(j)
        remote(outbox.at[peer[1]], final.at[me], fin_send.at[0], fin_recv.at[0], peer).start()
    final[me] = outbox[me]

    for step in range(LAST):
        here = block.at[0:3, core, :, 0:depth if step < LAST - 1 else half]
        remote(here, here, z_send.at[step], main_recv.at[0], sibling).wait_send()
    for step in range(LAST + 1):
        here = block.at[0:2, core, :, 0:half] if step < LAST else block.at[0:1, core, :, 0:half]
        remote(here, here, x_send.at[step], main_recv.at[0], sibling).wait_send()
    for b in range(LAST):
        sib_batch(b, 0, 4 if b else 2, 0, depth).wait_send()
    for k in range(QUARTERS):
        sib_batch(LAST + k, 0, 2, 0, quarter).wait_send()
    for b in range(LAST + 1):
        reduced(b, 0, 0, 256 if 0 < b < LAST else 128).wait_send()
    all_but_one = final.at[0:GROUP - 1]
    whole = remote(all_but_one, all_but_one, fin_send.at[0], fin_recv.at[0], sibling)
    whole.wait_send()
    whole.wait_recv()
    out_ref[...] = final[...].reshape(out_ref.shape).astype(jnp.float32)


def local(train_grads, query_grads, left_factor, right_factor, query_order):
    grads = train_grads[:, 0, :]
    raw = query_grads[:, 0, :]
    rows, depth = grads.shape
    own = raw.shape[0]
    queries = query_order.shape[0]
    dma = pltpu.SemaphoreType.DMA
    return pl.pallas_call(
        kernel,
        name="scores",
        out_shape=jax.ShapeDtypeStruct((rows, queries // GROUP), jnp.float32),
        in_specs=[pl.BlockSpec(memory_space=pl.ANY)] * 5,
        out_specs=pl.BlockSpec(memory_space=pltpu.VMEM),
        scratch_shapes=[
            pltpu.VMEM((own, depth), jnp.bfloat16),
            pltpu.VMEM((FA, FA), jnp.float32),
            pltpu.VMEM((FB, FB), jnp.float32),
            pltpu.VMEM((1, queries), jnp.int32),
            pltpu.VMEM((own * FA, FB), jnp.float32),
            pltpu.VMEM((own * FA, FB), jnp.float32),
            pltpu.VMEM((rows, depth), jnp.bfloat16),
            pltpu.VMEM((SLOTS, 2, own, depth), jnp.bfloat16),
            pltpu.VMEM((rows, 256), jnp.float32),
            pltpu.VMEM((rows, queries), jnp.bfloat16),
            pltpu.VMEM((queries, queries), jnp.bfloat16),
            pltpu.VMEM((rows // GROUP, queries), jnp.float32),
            pltpu.VMEM((GROUP - 1, rows // GROUP, queries), jnp.bfloat16),
            pltpu.VMEM((GROUP, rows // GROUP, queries // GROUP), jnp.bfloat16),
            pltpu.VMEM((GROUP, rows // GROUP, queries // GROUP), jnp.bfloat16),
            dma((5,)),
            dma((ARRIVALS,)),
            dma((LAST,)),
            dma((LAST + 1,)),
            dma((LAST + QUARTERS,)),
            dma((LAST + QUARTERS,)),
            dma((LAST + 1,)),
            dma((2,)),
            dma((1,)),
            dma((1,)),
        ],
        compiler_params=pltpu.CompilerParams(
            collective_id=0, has_side_effects=True, vmem_limit_bytes=60 * 2**20
        ),
        cost_estimate=pl.CostEstimate(
            flops=2 * rows * depth * queries, bytes_accessed=rows * depth * 2, transcendentals=0
        ),
    )(raw, grads, left_factor[0], right_factor[0], query_order.reshape(1, queries))


def solution(mesh):
    return jax.shard_map(
        local,
        mesh=mesh,
        in_specs=(
            P("ex", "layer", None),
            P("ex", "layer", None),
            P("layer", None, None),
            P("layer", None, None),
            P(),
        ),
        out_specs=P("ex", "layer"),
        check_vma=False,
    )
```

time: 225 us -> 88.5 us (0.39)
  waiting for transfers between devices: 183 us -> 0 us
  Pallas kernels: 0 us -> 86 us
  matrix products: 15.9 us -> 0 us
  between operations: 13.5 us -> 0.01 us
  local copies, waits for them, and re-layouts: 8.43 us -> 1.67 us
  other arithmetic: 4.13 us -> 0 us
    all_gather x1 -> x0, waiting for transfers between devices: 138 us -> none  [local(): lax.all_gather(outgoing, 'ex', axis=0, tiled=True)]
    pallas_call x0 -> x1, Pallas kernels: none -> 86 us  [local(): pl.pallas_call(kernel, name='scores', out_shape=jax.ShapeDtypeStruct((row...]
    reduce_scatter x1 -> x0, waiting for transfers between devices: 44.2 us -> none  [local(): summed = lax.psum_scatter(picked, 'layer', scatter_dimension=1, tiled=True)]
    dot_general x3 -> x0, matrix products: 15.9 us -> none  [the longest x1 14.4 us: local(): lax.dot_general(grads, lax.all_gather(outgoing, 'ex', axis=0, tiled=True)...]
    gather x1 -> x0, local copies, waits for them, and re-layouts: 4.85 us -> none  [local(): picked = jnp.take(tile, query_order, axis=1)]
    select_n x1 -> x0, other arithmetic: 3.15 us -> none  [local(): picked = jnp.take(tile, query_order, axis=1)]
  transfers between devices with their start and end apart: 2 -> 0, of which waited for: 2 -> 0; matrix products, arithmetic and copies ran while one was open for 0% -> 0% of each run, Pallas kernels for 0% -> 0%
where the time goes in v2:
time: 88.5 us; the launch traced here: 87.7 us
  Pallas kernels  86 us (97%)
  local copies, waits for them, and re-layouts  1.67 us (2%)
    pallas_call x1, Pallas kernels, local(): pl.pallas_call(kernel, name='scores', out_shape=jax.ShapeDtypeStruct((row...  86 us

profile of v2, /device:TPU:4, one launch (start us, length us, event | category | flops | bytes accessed | tf_op | source)
XLA Modules:
  0.0 87.7 jit_solution(13124458997512426521)
XLA Ops:
  0.0 86.0 %scores.1 = f32[512,128]{1,0:T(8,128)} custom-call(bf16[32,8192]{1,0:T(8,128)(2,1)} %bitcast.6, bf16[512,8192]{1,0:T(8,128)(2,1)} %bitcast.5, f32[64,64]{1,0:T(8,128)} %bitcast.8, f32[128,128]{1,0:T(8,128)} %bitcast.7, s32[1,1024]{1,0:T(1,128)} %bitcast.9), custom_call_target="tpu_custom_call" | custom-call | flops 8589934592 | bytes 8388608 | tf_op jit(solution)/shard_map/scores/pallas_call | solution.py:319
  86.0 1.7 %copy.7 = f32[512,128]{1,0:T(8,128)} copy(f32[512,128]{1,0:T(8,128)} %scores.1) | data formatting | bytes 524288

commit v3 on v0

v3 whole, which is shorter than its diff:
```python
import functools

import jax
import jax.numpy as jnp
from jax import lax
from jax.experimental import pallas as pl
from jax.experimental.pallas import tpu as pltpu
from jax.sharding import PartitionSpec as P

FA = 64
FB = 128
MESH = pl.DeviceIdType.MESH

Z = 8
GROUP = 8
FWD, BWD = 0, 1
WAYS = (FWD, BWD)

PIECES = (
    ("N", 0, 0), ("W", 0, 0), ("TW", 0, 0), ("TN", 0, 0), ("N", 1, 0), ("N", 1, 1), ("W", 1, 0), ("W", 1, 1),
    ("N", 2, 0), ("N", 2, 1), ("TW", 1, 0), ("TW", 1, 1), ("TN", 1, 0), ("TN", 1, 1), ("N", 3, 0), ("N", 3, 1),
    ("W", 2, 0), ("W", 2, 1), ("TN", 2, 0), ("TN", 2, 1), ("N", 4, 0), ("TW", 2, 0), ("TW", 2, 1), None,
    ("TN", 3, 0), ("TN", 3, 1), ("W", 3, 0), ("W", 3, 1), ("TN", 4, 0), None, None, None,
    ("TW", 3, 0), ("TW", 3, 1), ("W", 4, 0), ("TW", 4, 0),
)
BATCHES = ((0, 8), (8, 8), (16, 7), (24, 5), (32, 4))
FINAL = 35
NEAR_SUMS = 3
COLUMNS = 32 * len(PIECES)


def place(kind, step, way):
    return PIECES.index((kind, step, way if 0 < step < 4 else 0))


def batch_of(piece):
    return len(BATCHES) if piece == FINAL else piece // 8


SECOND = {place("N", 4, 0): 36, place("W", 4, 0): 37, place("TN", 4, 0): 38, FINAL: 39}
ARRIVALS = 42


def eye_plus(mat):
    n = mat.shape[0]
    rows = lax.broadcasted_iota(jnp.int32, (n, n), 0)
    cols = lax.broadcasted_iota(jnp.int32, (n, n), 1)
    return (jnp.where(rows == cols, 1.0, 0.0) + mat).astype(jnp.bfloat16)


def condition(raw, left_mat, right_mat, by_row, by_query, out):
    count = raw.shape[0]
    group = 16
    for a in range(0, FA, group):
        rows = jnp.concatenate([raw[:, i * FB:(i + 1) * FB] for i in range(a, a + group)], axis=0)
        mid = jnp.dot(rows, right_mat, preferred_element_type=jnp.float32).astype(jnp.bfloat16).astype(jnp.float32)
        for i in range(group):
            by_query[pl.ds(a + i, count, stride=FA), :] = mid[i * count:(i + 1) * count, :]
    group = 8
    for q in range(0, count, group):
        mid = jnp.concatenate([by_query[i * FA:(i + 1) * FA, :] for i in range(q, q + group)], axis=1)
        done = jnp.dot(left_mat, mid.astype(jnp.bfloat16), preferred_element_type=jnp.float32)
        for i in range(group):
            by_row[pl.ds(q + i, FA, stride=count), :] = done[:, i * FB:(i + 1) * FB]
    for a in range(FA):
        out[:, a * FB:(a + 1) * FB] = by_row[a * count:(a + 1) * count, :].astype(jnp.bfloat16)


def kernel(raw_ref, grads_ref, left_ref, right_ref, order_ref, out_ref, raw, left, right, order, by_row, by_query,
           grads, block, acc, tile, pick, scores, sums, halves, inbox, inbox_y, inbox_x, outbox, final,
           load_sem, main_recv, z_send, x_send, sib_send, sib_recv, red_send, red_recv, swap_send, swap_recv, fin_send, fin_recv):
    ex, me = lax.axis_index("ex"), lax.axis_index("layer")
    core = lax.rem(ex, 2)
    z = lax.rem(ex // 2, Z)
    hi = ex // (2 * Z)
    depth = block.shape[3]
    half, quarter = depth // 2, depth // 4

    def at(h, zz, c):
        return h * (2 * Z) + zz * 2 + c

    toward = ((at(hi, lax.rem(z + 1, Z), core), me), (at(hi, lax.rem(z + Z - 1, Z), core), me))
    across = (at(1 - hi, z, core), me)
    sibling = (at(hi, z, 1 - core), me)

    y, lo = lax.rem(me, 4), me // 4
    aside = (ex, lax.rem(me + 4, GROUP))

    def peer_of(j):
        return ex, lax.rem(me + j + 1, GROUP)

    def along_y(j):
        return ex, lo * 4 + lax.rem(y + j + 1, 4)

    def rows_of(device):
        return 2 * lax.rem(device[1], 4) + device[1] // 4

    loads = [pltpu.make_async_copy(src, dst, load_sem.at[i]) for i, (src, dst) in enumerate(
        ((raw_ref, raw), (right_ref, right), (left_ref, left), (order_ref, order), (grads_ref, grads)))]
    for load in loads[:4]:
        load.start()

    barrier = pltpu.get_barrier_semaphore()
    for d in (*toward, across, sibling):
        pl.semaphore_signal(barrier, inc=1, device_id=d, device_id_type=MESH)

    @pl.loop(0, GROUP - 1)
    def _(j):
        pl.semaphore_signal(barrier, inc=1, device_id=peer_of(j), device_id_type=MESH)

    for load in loads[:3]:
        load.wait()
    mats = eye_plus(left[...]), eye_plus(right[...])
    condition(raw.at[0:16], *mats, by_row, by_query, block.at[0, core])

    def remote(src, dst, send_sem, recv_sem, device):
        return pltpu.make_async_remote_copy(src_ref=src, dst_ref=dst, send_sem=send_sem, recv_sem=recv_sem,
                                            device_id=device, device_id_type=MESH)

    def part(piece, c, start, width):
        if width == depth:
            return block.at[piece, c]
        return block.at[piece, c, :, pl.ds(start if isinstance(start, int) else pl.multiple_of(start, width), width)]

    def send(src, dst, start, width, send_sem, signal, device):
        remote(part(src, core, start, width), part(dst, core, start, width), send_sem, main_recv.at[signal], device).start()

    def arrived(piece, start, width, signal):
        here = part(piece, core, start, width)
        remote(here, here, z_send.at[0], main_recv.at[signal], sibling).wait_recv()

    def send_sib(piece, start, width, group):
        here = part(piece, core, start, width)
        remote(here, here, sib_send.at[group], sib_recv.at[group], sibling).start()

    def round_z(kind, step, way):
        src, dst = place(kind, step, way), place(kind, step + 1, way)
        if step < 3:
            send(src, dst, 0, depth, z_send.at[step], dst, toward[way])
        elif dst != FINAL:
            send(src, dst, way * half, half, z_send.at[step], SECOND[dst] if way else dst, toward[way])
        else:
            for k in (2 * way, 2 * way + 1):
                send(src, dst, k * quarter, quarter, z_send.at[step], SECOND[dst] + k - 1 if k else dst, toward[way])

    def over_x(kind, step, way):
        src, dst = place(kind, step, way), place("T" + kind, step, way)
        if step < 4:
            send(src, dst, 0, depth, x_send.at[0], dst, across)
        else:
            send(src, dst, way * half, half, x_send.at[1], SECOND[dst] if way else dst, across)

    def take(kind, step, way):
        piece = place(kind, step, way)
        if step < 4:
            arrived(piece, 0, depth, piece)
            send_sib(piece, 0, depth, batch_of(piece))
        else:
            arrived(piece, way * half, half, SECOND[piece] if way else piece)
            send_sib(piece, way * half, half, batch_of(piece))

    def sib_batch(b):
        first, count = BATCHES[b]
        count -= b == len(BATCHES) - 1
        here = block.at[first:first + count, 1 - core]
        return remote(here, here, sib_send.at[b], sib_recv.at[b], sibling)

    def sib_last(k):
        here = part(FINAL, 1 - core, k * quarter, quarter)
        sem = len(BATCHES) + k
        return remote(here, here, sib_send.at[sem], sib_recv.at[sem], sibling)

    def product(first, count, start, width):
        cols = pl.ds(start if isinstance(start, int) else pl.multiple_of(start, width), width)
        rhs = block[first:first + count, :, :, cols].reshape(count * 32, width)
        return lax.dot_general(grads[:, cols], rhs, (((1,), (1,)), ((), ())), preferred_element_type=jnp.float32)

    def columns(b):
        first, count = BATCHES[b]
        return first * 32, 128 if count < 4 else 256

    def batch(b):
        first, count = BATCHES[b]
        sib_batch(b).wait_recv()
        w = count * 32
        acc[...] = jnp.zeros_like(acc)

        @pl.loop(0, 4)
        def _(i):
            k = i // 2 + 2 * lax.rem(i, 2)
            if b == len(BATCHES) - 1:
                sib_last(k).wait_recv()
            acc[:, :w] += product(first, count, k * quarter, quarter)
        start, width = columns(b)
        tile[:, start:start + w] = acc[:, :w].astype(jnp.bfloat16)

        cols = slice(start, start + width)
        if b >= NEAR_SUMS:
            to = slice(start - NEAR_SUMS * 256, start - NEAR_SUMS * 256 + width)

            @pl.loop(0, GROUP - 1)
            def _(j):
                peer = peer_of(j)
                rows = pl.ds(pl.multiple_of(rows_of(peer) * 64, 64), 64)
                remote(tile.at[rows, cols], inbox.at[j, :, to], red_send.at[b], red_recv.at[b], peer).start()
        else:
            @pl.loop(0, 3)
            def _(j):
                peer = along_y(j)
                rows = pl.ds(pl.multiple_of(lax.rem(peer[1], 4) * 128, 128), 128)
                remote(tile.at[rows, cols], inbox_y.at[j, :, cols], red_send.at[b], red_recv.at[b], peer).start()

    def reduced(b):
        start, width = columns(b)
        late = start - NEAR_SUMS * 256
        here = inbox.at[:, :, late:late + width] if b >= NEAR_SUMS else inbox_y.at[:, :, start:start + width]
        return remote(here, here, red_send.at[b], red_recv.at[b], sibling)

    def swap_x(b):
        start, width = columns(b)
        cols = slice(start, start + width)
        reduced(b).wait_recv()
        total = tile[pl.ds(pl.multiple_of(y * 128, 128), 128), cols].astype(jnp.float32)
        for j in range(3):
            total += inbox_y[j, :, cols].astype(jnp.float32)
        for i in range(2):
            sums[i, :, cols] = total[i * 64:(i + 1) * 64]
            halves[i, :, cols] = total[i * 64:(i + 1) * 64].astype(jnp.bfloat16)
        remote(halves.at[1 - lo, :, cols], inbox_x.at[:, cols], swap_send.at[b], swap_recv.at[0], aside).start()

    def swapped(start, width, b):
        here = inbox_x.at[:, start:start + width]
        return remote(here, here, swap_send.at[b], swap_recv.at[0], sibling)

    pl.semaphore_wait(barrier, 4 + GROUP - 1)
    for way in WAYS:
        round_z("N", 0, way)
    condition(raw.at[16:32], *mats, by_row, by_query, block.at[1, core])
    over_x("W", 0, 0)
    for way in WAYS:
        round_z("W", 0, way)
    for piece in (0, 1):
        send_sib(piece, 0, depth, 0)
    loads[4].start()

    loads[3].wait()
    row = lax.broadcasted_iota(jnp.int32, (32, 1), 0)
    row = row + 16 * (row // 16)

    def first_query(piece):
        kind, step, way = PIECES[piece]
        zz = lax.rem(z + (Z - step if way == FWD else step), Z)
        hh = 1 - hi if kind[0] == "T" else hi
        return (hh * Z + zz) * 64 + (16 if kind[-1] == "W" else 0)

    for piece in range(len(PIECES)):
        rows = slice(piece * 32, (piece + 1) * 32)
        if PIECES[piece] is None:
            pick[rows, :] = jnp.zeros((32, pick.shape[1]), jnp.bfloat16)
        else:
            pick[rows, :] = jnp.where(row + first_query(piece) == order[...], 1.0, 0.0).astype(jnp.bfloat16)
    tile[...] = jnp.zeros_like(tile)
    def ordered(total, start):
        high = total.astype(jnp.bfloat16)
        low = (total - high.astype(jnp.float32)).astype(jnp.bfloat16)
        both = jnp.dot(jnp.concatenate([high, low], axis=0), pick[start:start + total.shape[1], :],
                       preferred_element_type=jnp.float32)
        return both[:64] + both[64:]

    def late_sum(b):
        start, width = columns(b)
        reduced(b).wait_recv()
        total = tile[pl.ds(pl.multiple_of(rows_of((ex, me)) * 64, 64), 64), start:start + width].astype(jnp.float32)
        for j in range(GROUP - 1):
            total += inbox[j, :, start - NEAR_SUMS * 256:start - NEAR_SUMS * 256 + width].astype(jnp.float32)
        return ordered(total, start)

    for way in WAYS:
        take("N", 1, way)
        round_z("N", 1, way)
    over_x("N", 0, 0)
    for way in WAYS:
        over_x("N", 1, way)
    take("TW", 0, 0)
    for way in WAYS:
        round_z("TW", 0, way)
    for way in WAYS:
        take("W", 1, way)
    take("TN", 0, 0)
    loads[4].wait()
    batch(0)
    for way in WAYS:
        take("N", 2, way)
        round_z("N", 2, way)
        over_x("N", 2, way)
    for way in WAYS:
        round_z("W", 1, way)
    for kind in ("TW", "TN"):
        for way in WAYS:
            take(kind, 1, way)
    for way in WAYS:
        take("N", 3, way)
        round_z("N", 3, way)
        over_x("N", 3, way)
    for way in WAYS:
        round_z("TW", 1, way)
    swap_x(0)
    batch(1)
    for way in WAYS:
        take("W", 2, way)
        round_z("W", 2, way)
    for way in WAYS:
        take("N", 4, way)
        over_x("N", 4, way)
    for way in WAYS:
        take("TN", 2, way)
    for way in WAYS:
        take("TW", 2, way)
        round_z("TW", 2, way)
    swap_x(1)
    batch(2)
    for way in WAYS:
        take("W", 3, way)
        round_z("W", 3, way)
    for way in WAYS:
        take("TN", 3, way)
    for way in WAYS:
        take("TW", 3, way)
        round_z("TW", 3, way)
    for way in WAYS:
        take("TN", 4, way)
    swap_x(2)
    batch(3)
    for way in WAYS:
        take("W", 4, way)
    for k in (0, 2, 1, 3):
        arrived(FINAL, k * quarter, quarter, SECOND[FINAL] + k - 1 if k else FINAL)
        send_sib(FINAL, k * quarter, quarter, len(BATCHES) + k)
    batch(4)
    swapped(0, NEAR_SUMS * 256, 0).wait_recv()
    scores[...] = ordered(sums[lo] + inbox_x[...].astype(jnp.float32), 0)
    scores[...] += late_sum(3)
    done = (scores[...] + late_sum(4)).astype(jnp.bfloat16)
    for m in range(GROUP):
        outbox[m] = done[:, m * 128:(m + 1) * 128]

    @pl.loop(0, GROUP - 1)
    def _(j):
        peer = peer_of(j)
        remote(outbox.at[peer[1]], final.at[rows_of((ex, me))], fin_send.at[0], fin_recv.at[0], peer).start()
    final[rows_of((ex, me))] = outbox[me]

    def units(n, width, sem):
        here = block.at[0:n, core, :, 0:width]
        remote(here, here, sem, main_recv.at[0], sibling).wait_send()

    for step in range(4):
        units(6, depth if step < 3 else half, z_send.at[step])
    units(8, depth, x_send.at[0])
    units(2, half, x_send.at[1])
    for b in range(len(BATCHES)):
        sib_batch(b).wait_send()
        reduced(b).wait_send()
    for b in range(NEAR_SUMS):
        swapped(0, 256, b).wait_send()
    for k in range(4):
        sib_last(k).wait_send()
    whole = remote(final.at[0:GROUP - 1], final.at[0:GROUP - 1], fin_send.at[0], fin_recv.at[0], sibling)
    whole.wait_send()
    whole.wait_recv()
    out_ref[...] = final[...].reshape(out_ref.shape).astype(jnp.float32) * (1.0 / 256.0)


def local(train_grads, query_grads, left_factor, right_factor, query_order):
    grads = train_grads[:, 0, :]
    raw = query_grads[:, 0, :]
    rows, depth = grads.shape
    own = raw.shape[0]
    queries = query_order.shape[0]
    dma = pltpu.SemaphoreType.DMA
    return pl.pallas_call(
        kernel,
        name="scores",
        out_shape=jax.ShapeDtypeStruct((rows, queries // GROUP), jnp.float32),
        in_specs=[pl.BlockSpec(memory_space=pl.ANY)] * 5,
        out_specs=pl.BlockSpec(memory_space=pltpu.VMEM),
        scratch_shapes=[
            pltpu.VMEM((own, depth), jnp.bfloat16),
            pltpu.VMEM((FA, FA), jnp.float32),
            pltpu.VMEM((FB, FB), jnp.float32),
            pltpu.VMEM((1, queries), jnp.int32),
            pltpu.VMEM((own * FA, FB), jnp.float32),
            pltpu.VMEM((own * FA, FB), jnp.float32),
            pltpu.VMEM((rows, depth), jnp.bfloat16),
            pltpu.VMEM((len(PIECES), 2, own // 2, depth), jnp.bfloat16),
            pltpu.VMEM((rows, 256), jnp.float32),
            pltpu.VMEM((rows, COLUMNS), jnp.bfloat16),
            pltpu.VMEM((COLUMNS, queries), jnp.bfloat16),
            pltpu.VMEM((rows // GROUP, queries), jnp.float32),
            pltpu.VMEM((2, rows // GROUP, NEAR_SUMS * 256), jnp.float32),
            pltpu.VMEM((2, rows // GROUP, NEAR_SUMS * 256), jnp.bfloat16),
            pltpu.VMEM((GROUP - 1, rows // GROUP, COLUMNS - NEAR_SUMS * 256), jnp.bfloat16),
            pltpu.VMEM((3, rows // 4, NEAR_SUMS * 256), jnp.bfloat16),
            pltpu.VMEM((rows // GROUP, NEAR_SUMS * 256), jnp.bfloat16),
            pltpu.VMEM((GROUP, rows // GROUP, queries // GROUP), jnp.bfloat16),
            pltpu.VMEM((GROUP, rows // GROUP, queries // GROUP), jnp.bfloat16),
            dma((5,)),
            dma((ARRIVALS,)),
            dma((4,)),
            dma((2,)),
            dma((len(BATCHES) + 4,)),
            dma((len(BATCHES) + 4,)),
            dma((len(BATCHES),)),
            dma((len(BATCHES),)),
            dma((NEAR_SUMS,)),
            dma((1,)),
            dma((1,)),
            dma((1,)),
        ],
        compiler_params=pltpu.CompilerParams(
            collective_id=0, has_side_effects=True, vmem_limit_bytes=52 * 2**20
        ),
        cost_estimate=pl.CostEstimate(
            flops=2 * rows * depth * queries, bytes_accessed=rows * depth * 2, transcendentals=0
        ),
    )(*(pltpu.with_memory_space_constraint(x, pltpu.HBM) for x in (
        raw, grads, left_factor[0], right_factor[0], query_order.reshape(1, queries))))


def solution(mesh):
    return jax.shard_map(
        local,
        mesh=mesh,
        in_specs=(
            P("ex", "layer", None),
            P("ex", "layer", None),
            P("layer", None, None),
            P("layer", None, None),
            P(),
        ),
        out_specs=P("ex", "layer"),
        check_vma=False,
    )
```

time: 225 us -> 84.3 us (0.37)
  waiting for transfers between devices: 183 us -> 0 us
  Pallas kernels: 0 us -> 83.5 us
  matrix products: 15.9 us -> 0 us
  between operations: 13.5 us -> 0.01 us
  local copies, waits for them, and re-layouts: 8.43 us -> 0.71 us
  other arithmetic: 4.13 us -> 0 us
    all_gather x1 -> x0, waiting for transfers between devices: 138 us -> none  [local(): lax.all_gather(outgoing, 'ex', axis=0, tiled=True)]
    pallas_call x0 -> x1, Pallas kernels: none -> 83.5 us  [local(): pl.pallas_call(kernel, name='scores', out_shape=jax.ShapeDtypeStruct((row...]
    reduce_scatter x1 -> x0, waiting for transfers between devices: 44.2 us -> none  [local(): summed = lax.psum_scatter(picked, 'layer', scatter_dimension=1, tiled=True)]
    dot_general x3 -> x0, matrix products: 15.9 us -> none  [the longest x1 14.4 us: local(): lax.dot_general(grads, lax.all_gather(outgoing, 'ex', axis=0, tiled=True)...]
    gather x1 -> x0, local copies, waits for them, and re-layouts: 4.85 us -> none  [local(): picked = jnp.take(tile, query_order, axis=1)]
    select_n x1 -> x0, other arithmetic: 3.15 us -> none  [local(): picked = jnp.take(tile, query_order, axis=1)]
  transfers between devices with their start and end apart: 2 -> 0, of which waited for: 2 -> 0; matrix products, arithmetic and copies ran while one was open for 0% -> 0% of each run, Pallas kernels for 0% -> 0%
where the time goes in v3:
time: 84.3 us; the launch traced here: 84.2 us
  Pallas kernels  83.5 us (99%)
    pallas_call x1, Pallas kernels, local(): pl.pallas_call(kernel, name='scores', out_shape=jax.ShapeDtypeStruct((row...  83.5 us

profile of v3, /device:TPU:4, one launch (start us, length us, event | category | flops | bytes accessed | tf_op | source)
XLA Modules:
  0.0 84.2 jit_solution(14623856976958346484)
XLA Ops:
  0.0 83.5 %scores.1 = f32[512,128]{1,0:T(8,128)S(1)} custom-call(bf16[32,8192]{1,0:T(8,128)(2,1)} %bitcast.6, bf16[512,8192]{1,0:T(8,128)(2,1)} %bitcast.5, f32[64,64]{1,0:T(8,128)} %bitcast.8, f32[128,128]{1,0:T(8,128)} %bitcast.7, s32[1,1024]{1,0:T(1,128)} %bitcast.9), custom_call_target="tpu_custom_call" | custom-call | flops 8589934592 | bytes 8388608 | tf_op jit(solution)/shard_map/scores/pallas_call | solution.py:381
  83.5 0.7 copy.7

commit v4 on v3

--- a/solution.py
+++ b/solution.py
@@ -19,12 +19,11 @@
 PIECES = (
     ("N", 0, 0), ("W", 0, 0), ("TW", 0, 0), ("TN", 0, 0), ("N", 1, 0), ("N", 1, 1), ("W", 1, 0), ("W", 1, 1),
     ("N", 2, 0), ("N", 2, 1), ("TW", 1, 0), ("TW", 1, 1), ("TN", 1, 0), ("TN", 1, 1), ("N", 3, 0), ("N", 3, 1),
-    ("W", 2, 0), ("W", 2, 1), ("TN", 2, 0), ("TN", 2, 1), ("N", 4, 0), ("TW", 2, 0), ("TW", 2, 1), None,
-    ("TN", 3, 0), ("TN", 3, 1), ("W", 3, 0), ("W", 3, 1), ("TN", 4, 0), None, None, None,
-    ("TW", 3, 0), ("TW", 3, 1), ("W", 4, 0), ("TW", 4, 0),
+    ("W", 2, 0), ("W", 2, 1), ("TN", 2, 0), ("TN", 2, 1), ("N", 4, 0), ("TW", 2, 0), ("TW", 2, 1), ("W", 3, 0),
+    ("TN", 3, 0), ("TN", 3, 1), ("W", 3, 1), ("TW", 3, 0), ("TW", 3, 1), ("TN", 4, 0), ("W", 4, 0), ("TW", 4, 0),
 )
-BATCHES = ((0, 8), (8, 8), (16, 7), (24, 5), (32, 4))
-FINAL = 35
+BATCHES = ((0, 8), (8, 8), (16, 8), (24, 8))
+FINAL = 31
 NEAR_SUMS = 3
 COLUMNS = 32 * len(PIECES)
 
@@ -37,8 +36,15 @@
     return len(BATCHES) if piece == FINAL else piece // 8
 
 
-SECOND = {place("N", 4, 0): 36, place("W", 4, 0): 37, place("TN", 4, 0): 38, FINAL: 39}
-ARRIVALS = 42
+STRIP = 768
+
+SECOND = {place("N", 4, 0): 32, place("W", 4, 0): 33, place("TN", 4, 0): 34, FINAL: 35}
+STRIPS = {}
+for kind in ("W", "TW"):
+    for step in range(kind == "W", 5):
+        for way in WAYS if step else (FWD,):
+            STRIPS[kind, step, way] = 42 + len(STRIPS)
+ARRIVALS = 42 + len(STRIPS)
 
 
 def eye_plus(mat):
@@ -74,7 +80,8 @@
     z = lax.rem(ex // 2, Z)
     hi = ex // (2 * Z)
     depth = block.shape[3]
-    half, quarter = depth // 2, depth // 4
+    half, quarter, eighth = depth // 2, depth // 4, depth // 8
+    main = depth - STRIP
 
     def at(h, zz, c):
         return h * (2 * Z) + zz * 2 + c
@@ -133,31 +140,57 @@
         here = part(piece, core, start, width)
         remote(here, here, sib_send.at[group], sib_recv.at[group], sibling).start()
 
+    def strip_of(step, way):
+        return (main, STRIP) if step < 4 else (main + way * STRIP // 2, STRIP // 2)
+
+    def last_part(k):
+        if k < 6:
+            return k * eighth, eighth
+        return 6 * eighth + (k - 6) * (main - 6 * eighth) // 2, (main - 6 * eighth) // 2
+
+    def strip_round_z(step, way):
+        send(place("W", step, way), place("W", step + 1, way), *strip_of(step + 1, way), z_send.at[8 + step],
+             STRIPS["W", step + 1, way], toward[way])
+
     def round_z(kind, step, way):
         src, dst = place(kind, step, way), place(kind, step + 1, way)
-        if step < 3:
-            send(src, dst, 0, depth, z_send.at[step], dst, toward[way])
-        elif dst != FINAL:
-            send(src, dst, way * half, half, z_send.at[step], SECOND[dst] if way else dst, toward[way])
+        device = toward[way]
+        if kind == "N":
+            start, width = (0, depth) if step < 3 else (way * half, half)
+            send(src, dst, start, width, z_send.at[step], SECOND[dst] if step == 3 and way else dst, device)
+            if step > 0:
+                strip_round_z(step, way)
+        elif step < 3:
+            send(src, dst, 0, main, z_send.at[4 + step], dst, device)
+        elif kind == "W":
+            send(src, dst, way * main // 2, main // 2, z_send.at[4 + step], SECOND[dst] if way else dst, device)
         else:
-            for k in (2 * way, 2 * way + 1):
-                send(src, dst, k * quarter, quarter, z_send.at[step], SECOND[dst] + k - 1 if k else dst, toward[way])
+            for k in range(way, 8, 2):
+                send(src, dst, *last_part(k), z_send.at[4 + step], SECOND[dst] + k - 1 if k else dst, device)
 
     def over_x(kind, step, way):
         src, dst = place(kind, step, way), place("T" + kind, step, way)
-        if step < 4:
-            send(src, dst, 0, depth, x_send.at[0], dst, across)
-        else:
-            send(src, dst, way * half, half, x_send.at[1], SECOND[dst] if way else dst, across)
+        if kind == "W":
+            send(src, dst, 0, main, x_send.at[0], dst, across)
+            return
+        start, width = (0, depth) if step < 4 else (way * half, half)
+        send(src, dst, start, width, x_send.at[1 + step // 4], SECOND[dst] if step == 4 and way else dst, across)
+        send(place("W", step, way), place("TW", step, way), *strip_of(step, way), x_send.at[3 + step // 4],
+             STRIPS["TW", step, way], across)
 
     def take(kind, step, way):
         piece = place(kind, step, way)
-        if step < 4:
-            arrived(piece, 0, depth, piece)
-            send_sib(piece, 0, depth, batch_of(piece))
+        if kind[-1] == "W":
+            start, width = (0, main) if step < 4 else (way * main // 2, main // 2)
         else:
-            arrived(piece, way * half, half, SECOND[piece] if way else piece)
-            send_sib(piece, way * half, half, batch_of(piece))
+            start, width = (0, depth) if step < 4 else (way * half, half)
+        arrived(piece, start, width, SECOND[piece] if step == 4 and way else piece)
+        send_sib(piece, start, width, batch_of(piece))
+        if kind[-1] == "N":
+            wide = kind[:-1] + "W"
+            piece = place(wide, step, way)
+            arrived(piece, *strip_of(step, way), STRIPS[wide, step, way])
+            send_sib(piece, *strip_of(step, way), batch_of(piece) + 3 * (piece == FINAL))
 
     def sib_batch(b):
         first, count = BATCHES[b]
@@ -170,14 +203,18 @@
         sem = len(BATCHES) + k
         return remote(here, here, sib_send.at[sem], sib_recv.at[sem], sibling)
 
+    def take_last(i):
+        for k in (2 * i, 2 * i + 1):
+            arrived(FINAL, *last_part(k), SECOND[FINAL] + k - 1 if k else FINAL)
+            send_sib(FINAL, *last_part(k), len(BATCHES) + i)
+
     def product(first, count, start, width):
         cols = pl.ds(start if isinstance(start, int) else pl.multiple_of(start, width), width)
         rhs = block[first:first + count, :, :, cols].reshape(count * 32, width)
         return lax.dot_general(grads[:, cols], rhs, (((1,), (1,)), ((), ())), preferred_element_type=jnp.float32)
 
     def columns(b):
-        first, count = BATCHES[b]
-        return first * 32, 128 if count < 4 else 256
+        return b * 256, 256
 
     def batch(b):
         first, count = BATCHES[b]
@@ -186,11 +223,12 @@
         acc[...] = jnp.zeros_like(acc)
 
         @pl.loop(0, 4)
-        def _(i):
-            k = i // 2 + 2 * lax.rem(i, 2)
+        def _(k):
             if b == len(BATCHES) - 1:
                 sib_last(k).wait_recv()
             acc[:, :w] += product(first, count, k * quarter, quarter)
+            if b == len(BATCHES) - 1:
+                pl.when(k == 0)(lambda: take_last(3))
         start, width = columns(b)
         tile[:, start:start + w] = acc[:, :w].astype(jnp.bfloat16)
 
@@ -238,9 +276,11 @@
     condition(raw.at[16:32], *mats, by_row, by_query, block.at[1, core])
     over_x("W", 0, 0)
     for way in WAYS:
+        strip_round_z(0, way)
         round_z("W", 0, way)
     for piece in (0, 1):
         send_sib(piece, 0, depth, 0)
+    over_x("N", 0, 0)
     loads[4].start()
 
     loads[3].wait()
@@ -255,11 +295,7 @@
 
     for piece in range(len(PIECES)):
         rows = slice(piece * 32, (piece + 1) * 32)
-        if PIECES[piece] is None:
-            pick[rows, :] = jnp.zeros((32, pick.shape[1]), jnp.bfloat16)
-        else:
-            pick[rows, :] = jnp.where(row + first_query(piece) == order[...], 1.0, 0.0).astype(jnp.bfloat16)
-    tile[...] = jnp.zeros_like(tile)
+        pick[rows, :] = jnp.where(row + first_query(piece) == order[...], 1.0, 0.0).astype(jnp.bfloat16)
     def ordered(total, start):
         high = total.astype(jnp.bfloat16)
         low = (total - high.astype(jnp.float32)).astype(jnp.bfloat16)
@@ -278,7 +314,6 @@
     for way in WAYS:
         take("N", 1, way)
         round_z("N", 1, way)
-    over_x("N", 0, 0)
     for way in WAYS:
         over_x("N", 1, way)
     take("TW", 0, 0)
@@ -304,7 +339,6 @@
         over_x("N", 3, way)
     for way in WAYS:
         round_z("TW", 1, way)
-    swap_x(0)
     batch(1)
     for way in WAYS:
         take("W", 2, way)
@@ -317,30 +351,27 @@
     for way in WAYS:
         take("TW", 2, way)
         round_z("TW", 2, way)
+    for way in WAYS:
+        take("W", 3, way)
+        round_z("W", 3, way)
+    swap_x(0)
     swap_x(1)
     batch(2)
     for way in WAYS:
-        take("W", 3, way)
-        round_z("W", 3, way)
-    for way in WAYS:
         take("TN", 3, way)
     for way in WAYS:
         take("TW", 3, way)
         round_z("TW", 3, way)
-    for way in WAYS:
-        take("TN", 4, way)
+    for kind in ("W", "TN"):
+        for way in WAYS:
+            take(kind, 4, way)
+    for i in range(3):
+        take_last(i)
     swap_x(2)
     batch(3)
-    for way in WAYS:
-        take("W", 4, way)
-    for k in (0, 2, 1, 3):
-        arrived(FINAL, k * quarter, quarter, SECOND[FINAL] + k - 1 if k else FINAL)
-        send_sib(FINAL, k * quarter, quarter, len(BATCHES) + k)
-    batch(4)
     swapped(0, NEAR_SUMS * 256, 0).wait_recv()
     scores[...] = ordered(sums[lo] + inbox_x[...].astype(jnp.float32), 0)
-    scores[...] += late_sum(3)
-    done = (scores[...] + late_sum(4)).astype(jnp.bfloat16)
+    done = (scores[...] + late_sum(3)).astype(jnp.bfloat16)
     for m in range(GROUP):
         outbox[m] = done[:, m * 128:(m + 1) * 128]
 
@@ -355,9 +386,12 @@
         remote(here, here, sem, main_recv.at[0], sibling).wait_send()
 
     for step in range(4):
-        units(6, depth if step < 3 else half, z_send.at[step])
-    units(8, depth, x_send.at[0])
-    units(2, half, x_send.at[1])
+        parts = 1 if step < 3 else 2
+        units(2, depth // parts, z_send.at[step])
+        units(4, main // parts, z_send.at[4 + step])
+        units(2, STRIP // parts, z_send.at[8 + step])
+    for sem, (n, width) in enumerate(((1, main), (7, depth), (2, half), (7, STRIP), (2, STRIP // 2))):
+        units(n, width, x_send.at[sem])
     for b in range(len(BATCHES)):
         sib_batch(b).wait_send()
         reduced(b).wait_send()
@@ -406,8 +440,8 @@
             pltpu.VMEM((GROUP, rows // GROUP, queries // GROUP), jnp.bfloat16),
             dma((5,)),
             dma((ARRIVALS,)),
-            dma((4,)),
-            dma((2,)),
+            dma((12,)),
+            dma((5,)),
             dma((len(BATCHES) + 4,)),
             dma((len(BATCHES) + 4,)),
             dma((len(BATCHES),)),

time: 84.3 us -> 82.9 us (0.983)
  Pallas kernels: 83.5 us -> 82 us
    pallas_call x1, Pallas kernels: 83.5 us -> 82 us  [local(): pl.pallas_call(kernel, name='scores', out_shape=jax.ShapeDtypeStruct((row...]
where the time goes in v4:
time: 82.9 us; the launch traced here: 82.8 us
  Pallas kernels  82 us (99%)
    pallas_call x1, Pallas kernels, local(): pl.pallas_call(kernel, name='scores', out_shape=jax.ShapeDtypeStruct((row...  82 us

profile of v4, /device:TPU:4, one launch (start us, length us, event | category | flops | bytes accessed | tf_op | source)
XLA Modules:
  0.0 82.8 jit_solution(13971084689518592361)
XLA Ops:
  0.0 82.0 %scores.1 = f32[512,128]{1,0:T(8,128)S(1)} custom-call(bf16[32,8192]{1,0:T(8,128)(2,1)} %bitcast.6, bf16[512,8192]{1,0:T(8,128)(2,1)} %bitcast.5, f32[64,64]{1,0:T(8,128)} %bitcast.8, f32[128,128]{1,0:T(8,128)} %bitcast.7, s32[1,1024]{1,0:T(1,128)} %bitcast.9), custom_call_target="tpu_custom_call" | custom-call | flops 8589934592 | bytes 8388608 | tf_op jit(solution)/shard_map/scores/pallas_call | solution.py:415
  82.1 0.7 copy.7

commit v5 on v4

--- a/solution.py
+++ b/solution.py
@@ -138,7 +138,7 @@
 
     def send_sib(piece, start, width, group):
         here = part(piece, core, start, width)
-        remote(here, here, sib_send.at[group], sib_recv.at[group], sibling).start()
+        remote(here, here, sib_send.at[min(group, len(BATCHES))], sib_recv.at[group], sibling).start()
 
     def strip_of(step, way):
         return (main, STRIP) if step < 4 else (main + way * STRIP // 2, STRIP // 2)
@@ -149,7 +149,7 @@
         return 6 * eighth + (k - 6) * (main - 6 * eighth) // 2, (main - 6 * eighth) // 2
 
     def strip_round_z(step, way):
-        send(place("W", step, way), place("W", step + 1, way), *strip_of(step + 1, way), z_send.at[8 + step],
+        send(place("W", step, way), place("W", step + 1, way), *strip_of(step + 1, way), z_send.at[2],
              STRIPS["W", step + 1, way], toward[way])
 
     def round_z(kind, step, way):
@@ -157,16 +157,16 @@
         device = toward[way]
         if kind == "N":
             start, width = (0, depth) if step < 3 else (way * half, half)
-            send(src, dst, start, width, z_send.at[step], SECOND[dst] if step == 3 and way else dst, device)
+            send(src, dst, start, width, z_send.at[0], SECOND[dst] if step == 3 and way else dst, device)
             if step > 0:
                 strip_round_z(step, way)
         elif step < 3:
-            send(src, dst, 0, main, z_send.at[4 + step], dst, device)
+            send(src, dst, 0, main, z_send.at[1], dst, device)
         elif kind == "W":
-            send(src, dst, way * main // 2, main // 2, z_send.at[4 + step], SECOND[dst] if way else dst, device)
+            send(src, dst, way * main // 2, main // 2, z_send.at[1], SECOND[dst] if way else dst, device)
         else:
             for k in range(way, 8, 2):
-                send(src, dst, *last_part(k), z_send.at[4 + step], SECOND[dst] + k - 1 if k else dst, device)
+                send(src, dst, *last_part(k), z_send.at[1], SECOND[dst] + k - 1 if k else dst, device)
 
     def over_x(kind, step, way):
         src, dst = place(kind, step, way), place("T" + kind, step, way)
@@ -174,23 +174,25 @@
             send(src, dst, 0, main, x_send.at[0], dst, across)
             return
         start, width = (0, depth) if step < 4 else (way * half, half)
-        send(src, dst, start, width, x_send.at[1 + step // 4], SECOND[dst] if step == 4 and way else dst, across)
-        send(place("W", step, way), place("TW", step, way), *strip_of(step, way), x_send.at[3 + step // 4],
+        send(src, dst, start, width, x_send.at[1], SECOND[dst] if step == 4 and way else dst, across)
+        send(place("W", step, way), place("TW", step, way), *strip_of(step, way), x_send.at[2],
              STRIPS["TW", step, way], across)
 
-    def take(kind, step, way):
+    def take(kind, step, way, *onward):
         piece = place(kind, step, way)
         if kind[-1] == "W":
             start, width = (0, main) if step < 4 else (way * main // 2, main // 2)
         else:
             start, width = (0, depth) if step < 4 else (way * half, half)
         arrived(piece, start, width, SECOND[piece] if step == 4 and way else piece)
+        wide = place(kind[:-1] + "W", step, way)
+        if kind[-1] == "N":
+            arrived(wide, *strip_of(step, way), STRIPS[kind[:-1] + "W", step, way])
+        for go in onward:
+            go(kind, step, way)
         send_sib(piece, start, width, batch_of(piece))
         if kind[-1] == "N":
-            wide = kind[:-1] + "W"
-            piece = place(wide, step, way)
-            arrived(piece, *strip_of(step, way), STRIPS[wide, step, way])
-            send_sib(piece, *strip_of(step, way), batch_of(piece) + 3 * (piece == FINAL))
+            send_sib(wide, *strip_of(step, way), batch_of(wide) + 3 * (wide == FINAL))
 
     def sib_batch(b):
         first, count = BATCHES[b]
@@ -201,7 +203,7 @@
     def sib_last(k):
         here = part(FINAL, 1 - core, k * quarter, quarter)
         sem = len(BATCHES) + k
-        return remote(here, here, sib_send.at[sem], sib_recv.at[sem], sibling)
+        return remote(here, here, sib_send.at[len(BATCHES)], sib_recv.at[sem], sibling)
 
     def take_last(i):
         for k in (2 * i, 2 * i + 1):
@@ -278,8 +280,6 @@
     for way in WAYS:
         strip_round_z(0, way)
         round_z("W", 0, way)
-    for piece in (0, 1):
-        send_sib(piece, 0, depth, 0)
     over_x("N", 0, 0)
     loads[4].start()
 
@@ -312,10 +312,11 @@
         return ordered(total, start)
 
     for way in WAYS:
-        take("N", 1, way)
-        round_z("N", 1, way)
+        take("N", 1, way, round_z)
     for way in WAYS:
         over_x("N", 1, way)
+    for piece in (0, 1):
+        send_sib(piece, 0, depth, 0)
     take("TW", 0, 0)
     for way in WAYS:
         round_z("TW", 0, way)
@@ -325,49 +326,39 @@
     loads[4].wait()
     batch(0)
     for way in WAYS:
-        take("N", 2, way)
-        round_z("N", 2, way)
-        over_x("N", 2, way)
+        take("N", 2, way, round_z, over_x)
     for way in WAYS:
         round_z("W", 1, way)
     for kind in ("TW", "TN"):
         for way in WAYS:
             take(kind, 1, way)
     for way in WAYS:
-        take("N", 3, way)
-        round_z("N", 3, way)
-        over_x("N", 3, way)
+        take("N", 3, way, round_z, over_x)
     for way in WAYS:
         round_z("TW", 1, way)
     batch(1)
     for way in WAYS:
-        take("W", 2, way)
-        round_z("W", 2, way)
-    for way in WAYS:
-        take("N", 4, way)
-        over_x("N", 4, way)
+        take("W", 2, way, round_z)
+    for way in WAYS:
+        take("N", 4, way, over_x)
     for way in WAYS:
         take("TN", 2, way)
     for way in WAYS:
-        take("TW", 2, way)
-        round_z("TW", 2, way)
-    for way in WAYS:
-        take("W", 3, way)
-        round_z("W", 3, way)
-    swap_x(0)
-    swap_x(1)
+        take("TW", 2, way, round_z)
+    for way in WAYS:
+        take("W", 3, way, round_z)
     batch(2)
     for way in WAYS:
         take("TN", 3, way)
     for way in WAYS:
-        take("TW", 3, way)
-        round_z("TW", 3, way)
+        take("TW", 3, way, round_z)
     for kind in ("W", "TN"):
         for way in WAYS:
             take(kind, 4, way)
     for i in range(3):
         take_last(i)
-    swap_x(2)
+    for b in range(NEAR_SUMS):
+        swap_x(b)
     batch(3)
     swapped(0, NEAR_SUMS * 256, 0).wait_recv()
     scores[...] = ordered(sums[lo] + inbox_x[...].astype(jnp.float32), 0)
@@ -385,20 +376,16 @@
         here = block.at[0:n, core, :, 0:width]
         remote(here, here, sem, main_recv.at[0], sibling).wait_send()
 
-    for step in range(4):
-        parts = 1 if step < 3 else 2
-        units(2, depth // parts, z_send.at[step])
-        units(4, main // parts, z_send.at[4 + step])
-        units(2, STRIP // parts, z_send.at[8 + step])
-    for sem, (n, width) in enumerate(((1, main), (7, depth), (2, half), (7, STRIP), (2, STRIP // 2))):
+    for sem, (n, width) in enumerate(((7, depth), (14, main), (7, STRIP))):
+        units(n, width, z_send.at[sem])
+    for sem, (n, width) in enumerate(((1, main), (8, depth), (8, STRIP))):
         units(n, width, x_send.at[sem])
     for b in range(len(BATCHES)):
         sib_batch(b).wait_send()
         reduced(b).wait_send()
     for b in range(NEAR_SUMS):
         swapped(0, 256, b).wait_send()
-    for k in range(4):
-        sib_last(k).wait_send()
+    units(1, depth, sib_send.at[len(BATCHES)])
     whole = remote(final.at[0:GROUP - 1], final.at[0:GROUP - 1], fin_send.at[0], fin_recv.at[0], sibling)
     whole.wait_send()
     whole.wait_recv()
@@ -440,9 +427,9 @@
             pltpu.VMEM((GROUP, rows // GROUP, queries // GROUP), jnp.bfloat16),
             dma((5,)),
             dma((ARRIVALS,)),
-            dma((12,)),
-            dma((5,)),
-            dma((len(BATCHES) + 4,)),
+            dma((3,)),
+            dma((3,)),
+            dma((len(BATCHES) + 1,)),
             dma((len(BATCHES) + 4,)),
             dma((len(BATCHES),)),
             dma((len(BATCHES),)),

time: 82.9 us -> 82.7 us (level)
  no operation moved by 1% of the time
where the time goes in v5:
time: 82.7 us; the launch traced here: 82.6 us
  Pallas kernels  81.8 us (99%)
    pallas_call x1, Pallas kernels, local(): pl.pallas_call(kernel, name='scores', out_shape=jax.ShapeDtypeStruct((row...  81.8 us

profile of v5, /device:TPU:4, one launch (start us, length us, event | category | flops | bytes accessed | tf_op | source)
XLA Modules:
  0.0 82.6 jit_solution(9057454923092900645)
XLA Ops:
  0.0 81.8 %scores.1 = f32[512,128]{1,0:T(8,128)S(1)} custom-call(bf16[32,8192]{1,0:T(8,128)(2,1)} %bitcast.6, bf16[512,8192]{1,0:T(8,128)(2,1)} %bitcast.5, f32[64,64]{1,0:T(8,128)} %bitcast.8, f32[128,128]{1,0:T(8,128)} %bitcast.7, s32[1,1024]{1,0:T(1,128)} %bitcast.9), custom_call_target="tpu_custom_call" | custom-call | flops 8589934592 | bytes 8388608 | tf_op jit(solution)/shard_map/scores/pallas_call | solution.py:402
  81.9 0.7 copy.7

commit v6 on v4

--- a/solution.py
+++ b/solution.py
@@ -278,8 +278,6 @@
     for way in WAYS:
         strip_round_z(0, way)
         round_z("W", 0, way)
-    for piece in (0, 1):
-        send_sib(piece, 0, depth, 0)
     over_x("N", 0, 0)
     loads[4].start()
 
@@ -316,6 +314,8 @@
         round_z("N", 1, way)
     for way in WAYS:
         over_x("N", 1, way)
+    for piece in (0, 1):
+        send_sib(piece, 0, depth, 0)
     take("TW", 0, 0)
     for way in WAYS:
         round_z("TW", 0, way)

time: 82.9 us -> 82.9 us (level)
  no operation moved by 1% of the time
where the time goes in v6:
time: 82.9 us; the launch traced here: 82.8 us
  Pallas kernels  82 us (99%)
    pallas_call x1, Pallas kernels, local(): pl.pallas_call(kernel, name='scores', out_shape=jax.ShapeDtypeStruct((row...  82 us

profile of v6, /device:TPU:4, one launch (start us, length us, event | category | flops | bytes accessed | tf_op | source)
XLA Modules:
  0.0 82.8 jit_solution(11543077963460369460)
XLA Ops:
  0.0 82.0 %scores.1 = f32[512,128]{1,0:T(8,128)S(1)} custom-call(bf16[32,8192]{1,0:T(8,128)(2,1)} %bitcast.6, bf16[512,8192]{1,0:T(8,128)(2,1)} %bitcast.5, f32[64,64]{1,0:T(8,128)} %bitcast.8, f32[128,128]{1,0:T(8,128)} %bitcast.7, s32[1,1024]{1,0:T(1,128)} %bitcast.9), custom_call_target="tpu_custom_call" | custom-call | flops 8589934592 | bytes 8388608 | tf_op jit(solution)/shard_map/scores/pallas_call | solution.py:415
  82.1 0.7 copy.7
